TPU v7x, 32 devices: a whole 2x2x4 slice. The times are simulated.
32 devices in a mesh: row: 4 (over y, x), col: 8 (over z, core).
Axes of the slice: x: 2, y: 2, z: 4, core: 2. Of those that a mesh axis runs over, the one named last changes fastest.
Arguments:
- tile_values: bfloat16 [384, 2048, 256], P('row', 'col'), may hold values from -0.0546875 to 0.0546875
- tile_rows: int32 [384, 8], P('row', 'col'), may hold values from 0 to 15
- tile_cols: int32 [384, 8], P('row', 'col'), may hold values from 0 to 15
- objective: float32 [32768], P('col'), may hold values from -13 to 13
- demand: float32 [16384, 128], P(('row', 'col')), may hold values from -40 to 40
- lower_bound: float32 [32768], P('col'), may hold values from -1 to 0
- bound_span: float32 [32768], P('col'), may hold values from 0.2 to 2
- bound_types: int32 [32768], P('col'), may hold values from 0 to 2
- primal_start: float32 [32768, 128], P('col'), may hold values from -3 to 3
- dual_start: float32 [16384, 128], P(('row', 'col')), may hold values from -2 to 2
Outputs:
- primal: float32 [32768, 128], P('col')
- dual_final: float32 [16384, 128], P(('row', 'col'))
- primal_weight: float32 [128], replicated
Inputs may be any that keep to these rules, and one draw needn't show every extreme that they name: `tile_rows`: tile row of a tile inside its device's 16 tile rows; every device holds exactly 96 tiles and positions may repeat. `tile_cols`: tile column of a tile inside its device's 16 tile columns. `bound_types`: 0: free, 1: lower bound only, 2: both bounds.
All inputs are finite; a program needn't handle non-finite values.
Results may differ from a plain program's by a relative error of at most 0.0015.
Values may be sent and summed in bfloat16 or wider, within the bound.
A program may use at most 128 MiB of HBM per device.

v0:
```python
import jax
import jax.numpy as jnp
from jax import lax
from jax.sharding import PartitionSpec as P

ITERS = 2


eps_norm = 1e-06
step_scale = 0.4


def local_forward(tile_values, selector_rows, col_ids, mixed, count_cols):
    tile_size = tile_values.shape[1]
    width = mixed.shape[1]
    pieces = mixed.reshape(count_cols, tile_size, width)[col_ids]
    products = jnp.einsum("tij,tjs->tis", tile_values, pieces, preferred_element_type=jnp.float32)
    summed = jnp.einsum("rt,tis->ris", selector_rows, products, precision=lax.Precision.HIGHEST)
    return summed.reshape(selector_rows.shape[0] * tile_size, width)


def local_transpose(tile_values, selector_cols, row_ids, dual_rows, count_rows):
    tile_size = tile_values.shape[1]
    width = dual_rows.shape[1]
    pieces = dual_rows.reshape(count_rows, tile_size, width)[row_ids]
    products = jnp.einsum("tij,tis->tjs", tile_values, pieces, preferred_element_type=jnp.float32)
    summed = jnp.einsum("ct,tjs->cjs", selector_cols, products, precision=lax.Precision.HIGHEST)
    return summed.reshape(selector_cols.shape[0] * tile_size, width)


def project(value, lower_bound, bound_span, bound_types):
    low_edge = lower_bound[:, None]
    high_edge = low_edge + bound_span[:, None]
    bound_kind = bound_types[:, None]
    raised = jnp.maximum(value, low_edge)
    boxed = jnp.minimum(raised, high_edge)
    return jnp.where(bound_kind == 0, value, jnp.where(bound_kind == 1, raised, boxed))


def on_device(
    tile_values,
    tile_rows,
    tile_cols,
    objective,
    demand,
    lower_bound,
    bound_span,
    bound_types,
    primal_start,
    dual_start,
):
    n_col = lax.axis_size("col")
    col_pos = lax.axis_index("col")
    tile_size = tile_values.shape[1]
    share = dual_start.shape[0]
    count_rows = share * n_col // tile_size
    count_cols = primal_start.shape[0] // tile_size
    row_ids = tile_rows.reshape(-1)
    col_ids = tile_cols.reshape(-1)
    selector_rows = (jnp.arange(count_rows, dtype=jnp.int32)[:, None] == row_ids[None, :]).astype(
        jnp.float32
    )
    selector_cols = (jnp.arange(count_cols, dtype=jnp.int32)[:, None] == col_ids[None, :]).astype(
        jnp.float32
    )
    cost_local = jnp.sum(objective * objective)
    demand_local = jnp.sum(demand * demand, axis=0)
    cost_sq = lax.psum(cost_local, "col")
    demand_sq = lax.psum(demand_local, ("row", "col"))
    weight = jnp.sqrt(cost_sq + eps_norm) / jnp.sqrt(demand_sq + eps_norm)
    dual_full, demand_full = (
        lax.all_gather(dual_start, "col", axis=0, tiled=True),
        lax.all_gather(demand, "col", axis=0, tiled=True),
    )
    dual_rows = dual_full.astype(jnp.bfloat16)
    primal = primal_start
    for iteration in range(ITERS):
        step_primal = step_scale / weight
        step_dual = step_scale * weight
        pulled = lax.psum(
            local_transpose(tile_values, selector_cols, row_ids, dual_rows, count_rows), "row"
        )
        primal_next = project(
            primal - step_primal[None, :] * (objective[:, None] - pulled),
            lower_bound,
            bound_span,
            bound_types,
        )
        moved = primal_next - primal
        primal_local = jnp.sum(moved * moved, axis=0)
        mixed = (2.0 * primal_next - primal).astype(jnp.bfloat16)
        pushed_part = local_forward(tile_values, selector_rows, col_ids, mixed, count_cols)
        pushed = lax.psum(pushed_part, "col")
        change_full = step_dual[None, :] * (demand_full - pushed)
        dual_full = dual_full + change_full
        change = lax.dynamic_slice_in_dim(change_full, col_pos * share, share, 0)
        dual_rows = dual_full.astype(jnp.bfloat16)
        dual_local = jnp.sum(change * change, axis=0)
        primal_sq = lax.psum(primal_local, "col")
        dual_sq = lax.psum(dual_local, ("row", "col"))
        weight = jnp.sqrt(weight * jnp.sqrt((dual_sq + eps_norm) / (primal_sq + eps_norm)))
        primal = primal_next
    dual_final = lax.dynamic_slice_in_dim(dual_full, col_pos * share, share, 0)
    return (primal, dual_final, weight)


def solution(mesh):
    return jax.shard_map(
        on_device,
        mesh=mesh,
        in_specs=(
            P("row", "col", None),
            P("row", "col"),
            P("row", "col"),
            P("col"),
            P(("row", "col"), None),
            P("col"),
            P("col"),
            P("col"),
            P("col", None),
            P(("row", "col"), None),
        ),
        out_specs=(P("col", None), P(("row", "col"), None), P()),
        check_vma=False,
    )
```

profile of v0, /device:TPU:0, one launch (start us, length us, event | category | flops | bytes accessed | tf_op | source)
XLA Modules:
  0.0 543.3 jit_solution(9160699263512354210)
XLA Ops:
  7.2 0.0 all-gather.3.cloned.1.call-start
  7.2 0.7 all-gather.3.cloned.1.call-update
  7.9 0.0 all-reduce.5.cloned.1.call-start
  7.9 0.7 fusion.20
  8.6 32.8 %all-gather.3.cloned.1.call-done = f32[4096,128]{1,0:T(8,128)} async-done(((f32[512,128]{1,0:T(8,128)}), f32[4096,128]{1,0:T(8,128)}) %all-gather.3.cloned.1.call-update) | async-done | bytes 2097168 | tf_op jit(solution)/shard_map/all_gather | solution.py:72
  41.4 1.7 convert_element_type.14
  43.1 6.0 %gather_fusion = bf16[96,256,128]{2,1,0:T(8,128)(2,1)} fusion(bf16[16,256,128]{2,1,0:T(8,128)(2,1)S(1)} %bitcast.44, s32[1024]{0:T(1024)S(1)} %pad_clamp_fusion.1), kind=kCustom, calls=%fused_computation | custom fusion | bytes 12583296 | tf_op jit(solution)/shard_map/gather | solution.py:25
  49.1 13.2 %fusion.25 = f32[96,128,256]{2,1,0:T(8,128)} fusion(bf16[96,256,128]{2,1,0:T(8,128)(2,1)} %gather_fusion, bf16[96,256,256]{2,1,0:T(8,128)(2,1)} %param.10), kind=kOutput, calls=%fused_computation.53 | convolution fusion | flops 1610612736 | bytes 31457280 | tf_op jit(solution)/shard_map/tij,tis->tjs/dot_general | solution.py:26
  62.3 12.8 %copy.17 = f32[96,128,256]{1,0,2:T(8,128)} copy(f32[96,128,256]{2,1,0:T(8,128)} %fusion.25) | data formatting | bytes 25165824 | tf_op jit(solution)/shard_map/tij,tis->tjs/dot_general | solution.py:26
  75.0 0.0 copy-done.8
  75.1 7.1 %fusion.6 = f32[16,256,128]{2,0,1:T(8,128)S(1)} fusion(f32[96,128,256]{1,0,2:T(8,128)} %copy.17, s32[96]{0:T(128)S(1)} %bitcast.50), kind=kOutput, calls=%fused_computation.10 | convolution fusion | flops 603981312 | bytes 14680448 | tf_op jit(solution)/shard_map/ct,tjs->cjs/dot_general | solution.py:27
  82.1 2.0 copy.13
  84.1 0.0 copy-start.6
  84.1 0.0 all-reduce.5.cloned.1.call-update
  84.1 0.0 all-gather.5.cloned.1.call-start
  84.2 0.7 all-gather.5.cloned.1.call-update
  84.9 0.0 all-reduce.7.cloned.1.call-start
  84.9 0.0 copy-done.7
  85.0 0.0 copy-done.5
  85.0 0.6 multiply_reduce_fusion.5
  85.6 0.1 multiply_reduce_fusion.4
  85.7 16.0 %psum.70 = f32[]{:T(128)} all-reduce(f32[]{:T(128)} %multiply_reduce_fusion.5), channel_id=1, replica_groups=mesh['row'=4,'col'=8] {'col'}, use_global_device_ids=true, to_apply=%region_1.0 | all-reduce | flops 1 | bytes 8 | tf_op jit(solution)/shard_map/psum | solution.py:68
  102.3 38.2 %psum.71 = f32[128]{0:T(128)S(1)} all-reduce(f32[128]{0:T(128)S(1)} %multiply_reduce_fusion.4), channel_id=1, replica_groups=mesh['row'=4,'col'=8] {'row','col'}, use_global_device_ids=true, to_apply=%region_3.0 | all-reduce | flops 128 | bytes 1024 | tf_op jit(solution)/shard_map/psum | solution.py:69
  140.5 13.0 %all-reduce.5.cloned.1.call-done = f32[4096,128]{1,0:T(8,128)} async-done(((f32[4096,128]{1,0:T(8,128)}), f32[4096,128]{1,0:T(8,128)}) %all-reduce.5.cloned.1.call-update) | async-done | bytes 2097168 | tf_op jit(solution)/shard_map/psum | solution.py:80
  153.5 6.8 %multiply_reduce_fusion.1 = (f32[128]{0:T(128)S(1)}, f32[4096,128]{1,0:T(8,128)S(1)}) fusion(f32[4096,128]{1,0:T(8,128)} %param.18, f32[4096]{0:T(1024)S(1)} %add.67, f32[4096]{0:T(1024)S(1)} %copy-done.4, pred[4096]{0:T(1024)(128)(4,1)S(1)} %get-tuple-element.17, f32[4096,128]{1,0:T(8,128)} %all-reduce.5.cloned.1.call-done, f32[4096]{0:T(1024)S(1)} %copy-done.5, ...), kind=kLoop, calls=%fused_computation.19 | loop fusion | flops 5242752 | bytes 6349824 | tf_op jit(solution)/shard_map/reduce_sum | solution.py:90
  160.4 0.4 subtract_convert_fusion.1
  160.7 5.9 %gather_fusion.1 = bf16[96,256,128]{2,1,0:T(8,128)(2,1)} fusion(bf16[16,256,128]{2,1,0:T(8,128)(2,1)S(1)} %bitcast.45, s32[1024]{0:T(1024)S(1)} %pad_clamp_fusion), kind=kCustom, calls=%fused_computation.1 | custom fusion | bytes 12583296 | tf_op jit(solution)/shard_map/gather | solution.py:16
  166.7 11.2 %fusion.26 = f32[96,128,256]{2,1,0:T(8,128)} fusion(bf16[96,256,128]{2,1,0:T(8,128)(2,1)} %gather_fusion.1, bf16[96,256,256]{2,1,0:T(8,128)(2,1)} %param.10), kind=kOutput, calls=%fused_computation.54 | convolution fusion | flops 1610612736 | bytes 31457280 | tf_op jit(solution)/shard_map/tij,tjs->tis/dot_general | solution.py:17
  177.9 12.8 %copy.18 = f32[96,128,256]{1,0,2:T(8,128)} copy(f32[96,128,256]{2,1,0:T(8,128)} %fusion.26) | data formatting | bytes 25165824 | tf_op jit(solution)/shard_map/tij,tjs->tis/dot_general | solution.py:17
  190.7 7.1 %fusion.4 = f32[16,256,128]{2,0,1:T(8,128)S(1)} fusion(f32[96,128,256]{1,0,2:T(8,128)} %copy.18, s32[96]{0:T(128)S(1)} %bitcast.52), kind=kOutput, calls=%fused_computation.8 | convolution fusion | flops 603981312 | bytes 14680448 | tf_op jit(solution)/shard_map/rt,tis->ris/dot_general | solution.py:18
  197.8 2.0 copy.14
  199.8 0.0 all-reduce.7.cloned.1.call-update
  199.8 0.3 all-reduce.9.cloned.1.call-start
  200.0 0.0 all-gather.5.cloned.1.call-done
  200.1 64.7 %all-reduce.7.cloned.1.call-done = f32[4096,128]{1,0:T(8,128)} async-done(((f32[4096,128]{1,0:T(8,128)}), f32[4096,128]{1,0:T(8,128)}) %all-reduce.7.cloned.1.call-update) | async-done | bytes 2097168 | tf_op jit(solution)/shard_map/psum | solution.py:93
  264.7 5.3 fusion.24
  270.0 6.0 %gather_fusion.2 = bf16[96,256,128]{2,1,0:T(8,128)(2,1)} fusion(bf16[16,256,128]{2,1,0:T(8,128)(2,1)S(1)} %bitcast.42, s32[1024]{0:T(1024)S(1)} %pad_clamp_fusion.1), kind=kCustom, calls=%fused_computation.2 | custom fusion | bytes 12583296 | tf_op jit(solution)/shard_map/gather | solution.py:25
  276.0 13.2 %fusion.27 = f32[96,128,256]{2,1,0:T(8,128)} fusion(bf16[96,256,128]{2,1,0:T(8,128)(2,1)} %gather_fusion.2, bf16[96,256,256]{2,1,0:T(8,128)(2,1)} %param.10), kind=kOutput, calls=%fused_computation.55 | convolution fusion | flops 1610612736 | bytes 31457280 | tf_op jit(solution)/shard_map/tij,tis->tjs/dot_general | solution.py:26
  289.1 12.8 %copy.19 = f32[96,128,256]{1,0,2:T(8,128)} copy(f32[96,128,256]{2,1,0:T(8,128)} %fusion.27) | data formatting | bytes 25165824 | tf_op jit(solution)/shard_map/tij,tis->tjs/dot_general | solution.py:26
  301.9 7.1 %fusion.2 = f32[16,256,128]{2,0,1:T(8,128)S(1)} fusion(f32[96,128,256]{1,0,2:T(8,128)} %copy.19, s32[96]{0:T(128)S(1)} %bitcast.51), kind=kOutput, calls=%fused_computation.6 | convolution fusion | flops 603981312 | bytes 14680448 | tf_op jit(solution)/shard_map/ct,tjs->cjs/dot_general | solution.py:27
  309.0 1.9 copy.15
  310.9 0.0 all-reduce.9.cloned.1.call-update
  310.9 0.0 all-reduce.11.cloned.1.call-start
  311.0 13.6 %psum.75 = f32[128]{0:T(128)S(1)} all-reduce(f32[128]{0:T(128)S(1)} %get-tuple-element.7), channel_id=1, replica_groups=mesh['row'=4,'col'=8] {'col'}, use_global_device_ids=true, to_apply=%region_9.10 | all-reduce | flops 128 | bytes 1024 | tf_op jit(solution)/shard_map/psum | solution.py:99
  324.6 1.0 multiply_reduce_fusion.3
  325.6 38.3 %psum.74 = f32[128]{0:T(128)S(1)} all-reduce(f32[128]{0:T(128)S(1)} %multiply_reduce_fusion.3), channel_id=1, replica_groups=mesh['row'=4,'col'=8] {'row','col'}, use_global_device_ids=true, to_apply=%region_7.8 | all-reduce | flops 128 | bytes 1024 | tf_op jit(solution)/shard_map/psum | solution.py:100
  364.0 17.1 %all-reduce.9.cloned.1.call-done = f32[4096,128]{1,0:T(8,128)} async-done(((f32[4096,128]{1,0:T(8,128)}), f32[4096,128]{1,0:T(8,128)}) %all-reduce.9.cloned.1.call-update) | async-done | bytes 2097168 | tf_op jit(solution)/shard_map/psum | solution.py:80
  381.1 6.3 %multiply_reduce_fusion = (f32[128]{0:T(128)S(1)}, f32[4096,128]{1,0:T(8,128)S(1)}) fusion(f32[4096,128]{1,0:T(8,128)S(1)} %get-tuple-element.8, f32[4096]{0:T(1024)S(1)} %add.67, f32[4096]{0:T(1024)S(1)} %copy-done.4, pred[4096]{0:T(1024)(128)(4,1)S(1)} %get-tuple-element.17, f32[4096,128]{1,0:T(8,128)} %all-reduce.9.cloned.1.call-done, ...), kind=kLoop, calls=%fused_computation.16 | loop fusion | flops 5242752 | bytes 6349824 | tf_op jit(solution)/shard_map/reduce_sum | solution.py:90
  387.4 0.0 copy-start.2
  387.4 0.4 subtract_convert_fusion
  387.8 1.0 copy-done.2
  388.7 5.9 %gather_fusion.3 = bf16[96,256,128]{2,1,0:T(8,128)(2,1)} fusion(bf16[16,256,128]{2,1,0:T(8,128)(2,1)S(1)} %bitcast.43, s32[1024]{0:T(1024)S(1)} %pad_clamp_fusion), kind=kCustom, calls=%fused_computation.3 | custom fusion | bytes 12583296 | tf_op jit(solution)/shard_map/gather | solution.py:16
  394.7 11.1 %fusion.28 = f32[96,128,256]{2,1,0:T(8,128)} fusion(bf16[96,256,128]{2,1,0:T(8,128)(2,1)} %gather_fusion.3, bf16[96,256,256]{2,1,0:T(8,128)(2,1)} %param.10), kind=kOutput, calls=%fused_computation.56 | convolution fusion | flops 1610612736 | bytes 31457280 | tf_op jit(solution)/shard_map/tij,tjs->tis/dot_general | solution.py:17
  405.7 12.8 %copy.20 = f32[96,128,256]{1,0,2:T(8,128)} copy(f32[96,128,256]{2,1,0:T(8,128)} %fusion.28) | data formatting | bytes 25165824 | tf_op jit(solution)/shard_map/tij,tjs->tis/dot_general | solution.py:17
  418.5 7.1 %fusion = f32[16,256,128]{2,0,1:T(8,128)S(1)} fusion(f32[96,128,256]{1,0,2:T(8,128)} %copy.20, s32[96]{0:T(128)S(1)} %bitcast.53), kind=kOutput, calls=%fused_computation.4 | convolution fusion | flops 603981312 | bytes 14680448 | tf_op jit(solution)/shard_map/rt,tis->ris/dot_general | solution.py:18
  425.5 1.9 copy.16
  427.5 0.0 all-reduce.11.cloned.1.call-update
  427.5 16.8 %psum.79 = f32[128]{0:T(128)S(1)} all-reduce(f32[128]{0:T(128)S(1)} %get-tuple-element.3), channel_id=1, replica_groups=mesh['row'=4,'col'=8] {'col'}, use_global_device_ids=true, to_apply=%region_15.16 | all-reduce | flops 128 | bytes 1024 | tf_op jit(solution)/shard_map/psum | solution.py:99
  444.3 48.3 %all-reduce.11.cloned.1.call-done = f32[4096,128]{1,0:T(8,128)} async-done(((f32[4096,128]{1,0:T(8,128)}), f32[4096,128]{1,0:T(8,128)}) %all-reduce.11.cloned.1.call-update) | async-done | bytes 2097168 | tf_op jit(solution)/shard_map/psum | solution.py:93
  492.6 0.0 copy-done
  492.6 1.8 subtract_multiply_fusion
  494.4 1.7 multiply_reduce_fusion.2
  496.1 39.7 %psum.78 = f32[128]{0:T(128)S(1)} all-reduce(f32[128]{0:T(128)S(1)} %get-tuple-element.14), channel_id=1, replica_groups=mesh['row'=4,'col'=8] {'row','col'}, use_global_device_ids=true, to_apply=%region_13.14 | all-reduce | flops 128 | bytes 1024 | tf_op jit(solution)/shard_map/psum | solution.py:100
  535.9 0.5 multiply_sqrt_fusion
  (22 shorter events, 0.1 us)
Async XLA Ops:
  7.2 34.3 %all-gather.3.cloned.1.call-start = ((), (), s32[]{:S(2)}) async-start(), calls=%async_computation | async-start | bytes 2359296 | tf_op jit(solution)/shard_map/all_gather | solution.py:72
  7.9 145.6 %all-reduce.5.cloned.1.call-start = ((), (), s32[]{:S(2)}) async-start(), calls=%async_computation.1 | async-start | bytes 4194304 | tf_op jit(solution)/shard_map/psum | solution.py:80
  62.3 12.8 %copy-start.8 = (s32[96,1]{0,1:T(1,128)S(1)}, s32[96,1]{0,1:T(1,128)}, u32[]{:S(2)}) copy-start(s32[96,1]{0,1:T(1,128)} %param.12) | copy-start | bytes 1156
  84.1 0.8 copy-start.7
  84.1 0.9 copy-start.5
  84.1 1.5 copy-start.3
  84.1 56.4 %copy-start.4 = (f32[4096]{0:T(1024)S(1)}, f32[4096]{0:T(1024)}, u32[]{:S(2)}) copy-start(f32[4096]{0:T(1024)} %param.15) | copy-start | bytes 49156
  84.1 56.4 %copy-start.6 = (f32[4096]{0:T(1024)S(1)}, f32[4096]{0:T(1024)}, u32[]{:S(2)}) copy-start(f32[4096]{0:T(1024)} %param.16) | copy-start | bytes 49156
  84.1 115.9 %all-gather.5.cloned.1.call-start = ((), (), s32[]{:S(2)}) async-start(), calls=%async_computation.2 | async-start | bytes 2359296 | tf_op jit(solution)/shard_map/all_gather | solution.py:73
  84.9 179.9 %all-reduce.7.cloned.1.call-start = ((), (), s32[]{:S(2)}) async-start(), calls=%async_computation.3 | async-start | bytes 4194304 | tf_op jit(solution)/shard_map/psum | solution.py:93
  153.5 6.8 %copy-start.1 = (f32[4096,128]{1,0:T(8,128)S(1)}, f32[4096,128]{1,0:T(8,128)}, u32[]{:S(2)}) copy-start(f32[4096,128]{1,0:T(8,128)} %param.18) | copy-start | bytes 6291460
  177.9 12.8 %copy-start.9 = (s32[96,1]{0,1:T(1,128)S(1)}, s32[96,1]{0,1:T(1,128)}, u32[]{:S(2)}) copy-start(s32[96,1]{0,1:T(1,128)} %param.11) | copy-start | bytes 1156
  199.8 181.3 %all-reduce.9.cloned.1.call-start = ((), (), s32[]{:S(2)}) async-start(), calls=%async_computation.4 | async-start | bytes 4194304 | tf_op jit(solution)/shard_map/psum | solution.py:80
  310.9 181.7 %all-reduce.11.cloned.1.call-start = ((), (), s32[]{:S(2)}) async-start(), calls=%async_computation.5 | async-start | bytes 4194304 | tf_op jit(solution)/shard_map/psum | solution.py:93
  387.4 1.3 copy-start.2
  427.5 65.2 %copy-start = (f32[4096,128]{1,0:T(8,128)S(1)}, f32[4096,128]{1,0:T(8,128)}, u32[]{:S(2)}) copy-start(f32[4096,128]{1,0:T(8,128)} %all-gather.5.cloned.1.call-done) | copy-start | bytes 6291460
Sparse Core Ops, SparseCore 0:
  9.6 31.7 all-gather.2
  84.3 69.2 all-reduce.4
  155.2 29.0 all-gather.4
  199.9 64.7 all-reduce.6
  311.1 69.9 all-reduce.8
  427.6 64.9 all-reduce.10
where the time goes:
time: 545 us; the launch traced here: 543 us
  waiting for transfers between devices  177 us (32%)
  blocking collectives  163 us (30%)
  local copies, waits for them, and re-layouts  83.7 us (15%)
  matrix products  76.9 us (14%)
  other arithmetic  27.3 us (5%)
  between operations  15 us (3%)
    psum x2, waiting for transfers between devices, on_device(): pushed = lax.psum(pushed_part, 'col')  113 us
    psum x2, blocking collectives, on_device(): dual_sq = lax.psum(dual_local, ('row', 'col'))  78 us
    psum x1, blocking collectives, on_device(): demand_sq = lax.psum(demand_local, ('row', 'col'))  38.2 us
    all_gather x1, waiting for transfers between devices, on_device(): lax.all_gather(dual_start, 'col', axis=0, tiled=True)  32.8 us
    psum x2, blocking collectives, on_device(): primal_sq = lax.psum(primal_local, 'col')  30.4 us
    psum x2, waiting for transfers between devices, on_device(): lax.psum(local_transpose(tile_values, selector_cols, row_ids, dual_rows,...  30.1 us
    dot_general x2, matrix products, local_transpose(): jnp.einsum('tij,tis->tjs', tile_values, pieces, preferred_element_type=jn...  26.4 us
    dot_general x2, local copies, waits for them, and re-layouts, local_forward(): jnp.einsum('tij,tjs->tis', tile_values, pieces, preferred_element_type=jn...  25.6 us
  transfers between devices with their start and end apart: 6, of which 5 were waited for; matrix products, arithmetic and copies ran while one was open for 9% of the time, Pallas kernels for 0%

commit v1 on v0

v1 whole, which is shorter than its diff:
```python
import functools
import jax
import jax.numpy as jnp
from jax import lax
from jax.experimental import pallas as pl
from jax.experimental.pallas import tpu as pltpu
from jax.sharding import PartitionSpec as P

ITERS = 2
CORES = 2

eps_norm = 1e-06
step_scale = 0.4
MESH = pl.DeviceIdType.MESH


def schedule(keys, others, count):
    total = keys.shape[0]
    order = jnp.arange(total, dtype=jnp.int32)
    ahead = (keys[None, :] < keys[:, None]) | (
        (keys[None, :] == keys[:, None]) & (order[None, :] < order[:, None])
    )
    rank = jnp.sum(ahead.astype(jnp.int32), axis=1)
    here = rank[None, :] == order[:, None]
    perm = jnp.sum(jnp.where(here, order[None, :], 0), axis=1)
    other = jnp.sum(jnp.where(here, others[None, :], 0), axis=1)
    first = here & ~jnp.any(
        (keys[None, :] == keys[:, None]) & (order[None, :] < order[:, None]), axis=1
    )[None, :]
    keep = 1 - jnp.sum(first.astype(jnp.int32), axis=1)
    ids = jnp.arange(count, dtype=jnp.int32)
    cnt = jnp.sum((keys[None, :] == ids[:, None]).astype(jnp.int32), axis=1)
    upto = jnp.sum((keys[None, :] <= ids[:, None]).astype(jnp.int32), axis=1)
    return jnp.stack([perm, other, keep]), jnp.stack([jnp.maximum(upto - 1, 0), cnt])


def kernel(
    n_row, n_col,
    plan_r, plan_c, ends_r, ends_c, tiles_any, params, demand, primal_any, dual_start,
    primal_out, dual_out, weight_out,
    tiles, primal, dual_rows, dual_t, run, pull_out, pull_own, pull_in, mixed,
    pair_out, pair_in, push_out, push_own, push_in, norm_row, norm_col,
    load_sem, gather_send, gather_recv, pass_send, pull_send, pull_recv,
    mix_send, mix_recv, final_send, final_recv, pair_send, pair_recv,
    push_send, push_recv, nrow_send, nrow_recv, ncol_send, ncol_recv,
):
    i, j = lax.axis_index("row"), lax.axis_index("col")
    n_chip = n_col // CORES
    chip, core = lax.div(j, CORES), lax.rem(j, CORES)
    other_core = 1 - core
    partner = (i, chip * CORES + other_core)
    total, size = tiles.shape[0], tiles.shape[1]
    share = demand.shape[0]
    quarter = primal.shape[0]
    blocks_c = n_row * quarter
    blocks_r = n_col * share
    width = demand.shape[2]
    half = size // 2
    sends = []

    def remote(src, dst, send_sem, recv_sem, device):
        return pltpu.make_async_remote_copy(
            src_ref=src, dst_ref=dst, send_sem=send_sem, recv_sem=recv_sem,
            device_id=device, device_id_type=MESH,
        )

    def send(*args):
        copy = remote(*args)
        copy.start()
        sends.append(copy)

    row_peer = [lax.rem(i + d, n_row) for d in range(n_row)]
    col_peer = [lax.rem(j + d, n_col) for d in range(n_col)]
    chip_peer = [lax.rem(chip + d, n_chip) for d in range(n_chip)]

    load_tiles = pltpu.make_async_copy(tiles_any, tiles, load_sem.at[0])
    load_tiles.start()
    load_primal = pltpu.make_async_copy(
        primal_any.at[pl.ds(i * quarter, quarter)], primal, load_sem.at[1]
    )
    load_primal.start()

    barrier = pltpu.get_barrier_semaphore()
    for d in range(1, n_row):
        pl.semaphore_signal(barrier, inc=1, device_id=(row_peer[d], j), device_id_type=MESH)
    for d in range(1, n_col):
        pl.semaphore_signal(barrier, inc=1, device_id=(i, col_peer[d]), device_id_type=MESH)
    pl.semaphore_wait(barrier, n_row + n_col - 2)

    def share_of(t, owner):
        return dual_rows.at[pl.ds(t * blocks_r + owner * share, share)]

    def gather_start(t):
        for d in range(1, n_chip):
            send(share_of(t, j), share_of(t, j), gather_send.at[t, d], gather_recv.at[t, j],
                 (i, chip_peer[d] * CORES + core))
        send(share_of(t, j), share_of(t, j), pass_send.at[t, 0], gather_recv.at[t, j], partner)

    def gather_finish(t):
        for d in range(1, n_chip):
            owner = chip_peer[n_chip - d] * CORES + core
            remote(share_of(t, owner), share_of(t, owner), gather_send.at[t, d],
                   gather_recv.at[t, owner], partner).wait_recv()
            send(share_of(t, owner), share_of(t, owner), pass_send.at[t, d],
                 gather_recv.at[t, owner], partner)
        for d in range(n_chip):
            owner = chip_peer[d] * CORES + other_core
            remote(share_of(t, owner), share_of(t, owner), pass_send.at[t, d],
                   gather_recv.at[t, owner], partner).wait_recv()

    def norm_start(t, first, second):
        norm_row[t * n_row + i] = jnp.concatenate(
            [first, second, jnp.zeros((6, width), jnp.float32)], axis=0
        )
        for d in range(1, n_row):
            slot = norm_row.at[t * n_row + i]
            send(slot, slot, nrow_send.at[t, d], nrow_recv.at[t, i], (row_peer[d], j))

    def norm_middle(t):
        for d in range(1, n_row):
            slot = norm_row.at[t * n_row + row_peer[d]]
            remote(slot, slot, nrow_send.at[t, d], nrow_recv.at[t, row_peer[d]],
                   (row_peer[d], j)).wait_recv()
        added = norm_row[t * n_row]
        for k in range(1, n_row):
            added = added + norm_row[t * n_row + k]
        norm_col[t * n_col + j] = added
        for d in range(1, n_col):
            slot = norm_col.at[t * n_col + j]
            send(slot, slot, ncol_send.at[t, d], ncol_recv.at[t, j], (i, col_peer[d]))

    def norm_finish(t):
        for d in range(1, n_col):
            slot = norm_col.at[t * n_col + col_peer[d]]
            remote(slot, slot, ncol_send.at[t, d], ncol_recv.at[t, col_peer[d]],
                   (i, col_peer[d])).wait_recv()
        added = norm_col[t * n_col]
        for k in range(1, n_col):
            added = added + norm_col[t * n_col + k]
        return added[0:1, :], added[1:2, :]

    zero_row = jnp.zeros((1, width), jnp.float32)

    def start_block(b, carry):
        value = dual_start[b]
        dual_out[b] = value
        dual_rows[j * share + b] = value.astype(jnp.bfloat16)
        wanted = demand[b]
        return carry + jnp.sum(wanted * wanted, axis=0, keepdims=True)

    demand_sq = lax.fori_loop(0, share, start_block, zero_row)
    gather_start(0)
    cost = params[:, 0:1]
    cost_sq = jnp.sum(cost * cost, axis=0, keepdims=True)
    norm_start(0, demand_sq, jnp.broadcast_to(cost_sq, (1, width)))
    norm_middle(0)
    weight = None
    load_primal.wait()
    load_tiles.wait()

    for t in range(ITERS):
        gather_finish(t)
        if t > 0:
            norm_middle(t)

        def turn(b, carry):
            dual_t[b] = dual_rows[t * blocks_r + b].astype(jnp.float32).T.astype(jnp.bfloat16)
            return carry

        lax.fori_loop(0, blocks_r, turn, 0)

        def pull_tile(n, before):
            added = jnp.dot(dual_t[plan_c[1, n]], tiles[plan_c[0, n]],
                            preferred_element_type=jnp.float32)
            added = added + jnp.where(plan_c[2, n] == 1, before, 0.0)
            run[n, 0:half, :] = added[:, 0:half]
            run[n, half:size, :] = added[:, half:size]
            return added

        lax.fori_loop(0, total, pull_tile, jnp.zeros((width, size), jnp.float32), unroll=4)

        def pulled_block(block, row):
            last = ends_c[0, block]
            held = ends_c[1, block] > 0
            return jnp.where(held, run[last, row:row + half, :], 0.0).T

        for d in range(1, n_row):
            dest = row_peer[d]

            def pack_pull(b, carry):
                at = dest * quarter + b
                for row in (0, half):
                    pull_out[t * blocks_c + at, row:row + half, :] = pulled_block(at, row).astype(
                        jnp.bfloat16)
                return carry

            lax.fori_loop(0, quarter, pack_pull, 0)
            send(pull_out.at[pl.ds(t * blocks_c + dest * quarter, quarter)],
                 pull_in.at[pl.ds(t * blocks_c + i * quarter, quarter)],
                 pull_send.at[t, d], pull_recv.at[t, i], (dest, j))

        def keep_pull(b, carry):
            for row in (0, half):
                pull_own[b, row:row + half, :] = pulled_block(i * quarter + b, row)
            return carry

        lax.fori_loop(0, quarter, keep_pull, 0)

        if t == 0:
            demand_all, cost_all = norm_finish(0)
            weight = jnp.sqrt(cost_all + eps_norm) / jnp.sqrt(demand_all + eps_norm)
        else:
            dual_all, primal_all = norm_finish(t)
            weight = jnp.sqrt(weight * jnp.sqrt((dual_all + eps_norm) / (primal_all + eps_norm)))
        step_primal = step_scale / weight
        step_dual = step_scale * weight

        for d in range(1, n_row):
            origin = row_peer[n_row - d]
            slot = pull_in.at[pl.ds(t * blocks_c + origin * quarter, quarter)]
            remote(slot, slot, pull_send.at[t, d], pull_recv.at[t, origin],
                   (origin, j)).wait_recv()

        def update_primal(b, carry):
            pulled = pull_own[b]
            for d in range(1, n_row):
                pulled = pulled + pull_in[
                    t * blocks_c + row_peer[d] * quarter + b].astype(jnp.float32)
            rows = pl.ds(pl.multiple_of(b * size, size), size)
            old = primal[b]
            value = old - step_primal * (params[rows, 0:1] - pulled)
            new = jnp.minimum(jnp.maximum(value, params[rows, 1:2]), params[rows, 2:3])
            moved = new - old
            mixed[t * blocks_c + i * quarter + b] = (2.0 * new - old).astype(jnp.bfloat16)
            if t == ITERS - 1:
                primal_out[i * quarter + b] = new
            else:
                primal[b] = new
            return carry + jnp.sum(moved * moved, axis=0, keepdims=True)

        primal_sq = lax.fori_loop(0, quarter, update_primal, zero_row)

        mine = mixed.at[pl.ds(t * blocks_c + i * quarter, quarter)]
        for d in range(1, n_row):
            send(mine, mine, mix_send.at[t, d], mix_recv.at[t, i], (row_peer[d], j))
        for d in range(1, n_row):
            origin = row_peer[n_row - d]
            slot = mixed.at[pl.ds(t * blocks_c + origin * quarter, quarter)]
            remote(slot, slot, mix_send.at[t, d], mix_recv.at[t, origin],
                   (origin, j)).wait_recv()
        if t == ITERS - 1:
            mine = primal_out.at[pl.ds(i * quarter, quarter)]
            for d in range(1, n_row):
                send(mine, mine, final_send.at[d], final_recv.at[i], (row_peer[d], j))

        def push_tile(n, before):
            added = jnp.dot(tiles[plan_r[0, n]], mixed[t * blocks_c + plan_r[1, n]],
                            preferred_element_type=jnp.float32)
            added = added + jnp.where(plan_r[2, n] == 1, before, 0.0)
            run[n] = added
            return added

        lax.fori_loop(0, total, push_tile, jnp.zeros((size, width), jnp.float32), unroll=4)

        def pushed_block(block):
            return jnp.where(ends_r[1, block] > 0, run[ends_r[0, block]], 0.0)

        def part(ref, owner_chip):
            return ref.at[pl.ds((t * n_chip + owner_chip) * share, share)]

        order = [*range(1, n_chip), 0]
        for d in order:
            dest = chip_peer[d]

            def pack_pair(b, carry):
                pair_out[(t * n_chip + dest) * share + b] = pushed_block(
                    (dest * CORES + other_core) * share + b).astype(pair_out.dtype)
                return carry

            lax.fori_loop(0, share, pack_pair, 0)
            send(part(pair_out, dest), part(pair_in, dest), pair_send.at[t, d],
                 pair_recv.at[t, dest], partner)
        for d in order:
            dest = chip_peer[d]
            slot = part(pair_in, dest)
            remote(slot, slot, pair_send.at[t, d], pair_recv.at[t, dest], partner).wait_recv()

            def pack_push(b, carry):
                at = (t * n_chip + dest) * share + b
                value = pushed_block((dest * CORES + core) * share + b) + pair_in[at].astype(
                    jnp.float32)
                if d == 0:
                    push_own[b] = value
                else:
                    push_out[at] = value.astype(jnp.bfloat16)
                return carry

            lax.fori_loop(0, share, pack_push, 0)
            if d != 0:
                send(part(push_out, dest), part(push_in, chip), push_send.at[t, d],
                     push_recv.at[t, chip], (i, dest * CORES + core))
        for d in range(1, n_chip):
            origin = chip_peer[n_chip - d]
            slot = part(push_in, origin)
            remote(slot, slot, push_send.at[t, d], push_recv.at[t, origin],
                   (i, origin * CORES + core)).wait_recv()

        def update_dual(b, carry):
            pushed = push_own[b]
            for d in range(1, n_chip):
                pushed = pushed + push_in[
                    (t * n_chip + chip_peer[d]) * share + b].astype(jnp.float32)
            change = step_dual * (demand[b] - pushed)
            new = dual_out[b] + change
            dual_out[b] = new
            if t < ITERS - 1:
                dual_rows[(t + 1) * blocks_r + j * share + b] = new.astype(jnp.bfloat16)
            return carry + jnp.sum(change * change, axis=0, keepdims=True)

        dual_sq = lax.fori_loop(0, share, update_dual, zero_row)
        norm_start(t + 1, dual_sq, primal_sq)
        if t < ITERS - 1:
            gather_start(t + 1)

    norm_middle(ITERS)
    dual_all, primal_all = norm_finish(ITERS)
    weight = jnp.sqrt(weight * jnp.sqrt((dual_all + eps_norm) / (primal_all + eps_norm)))
    weight_out[...] = jnp.broadcast_to(weight, weight_out.shape)
    for d in range(1, n_row):
        origin = row_peer[n_row - d]
        slot = primal_out.at[pl.ds(origin * quarter, quarter)]
        remote(slot, slot, final_send.at[d], final_recv.at[origin], (origin, j)).wait_recv()
    for copy in sends:
        copy.wait_send()


def on_device(
    tile_values, tile_rows, tile_cols, objective, demand, lower_bound, bound_span, bound_types,
    primal_start, dual_start,
):
    n_row, n_col = lax.axis_size("row"), lax.axis_size("col")
    total, size = tile_values.shape[0], tile_values.shape[1]
    width = demand.shape[1]
    share = dual_start.shape[0] // size
    blocks_r = share * n_col
    blocks_c = primal_start.shape[0] // size
    quarter = blocks_c // n_row
    n_chip = n_col // CORES
    row_ids, col_ids = tile_rows.reshape(-1), tile_cols.reshape(-1)
    plan_r, ends_r = schedule(row_ids, col_ids, blocks_r)
    plan_c, ends_c = schedule(col_ids, row_ids, blocks_c)
    low = jnp.where(bound_types == 0, -jnp.inf, lower_bound)
    high = jnp.where(bound_types == 2, lower_bound + bound_span, jnp.inf)
    params = lax.dynamic_slice_in_dim(
        jnp.stack([objective, low, high, jnp.zeros_like(low)], axis=1),
        lax.axis_index("row") * quarter * size, quarter * size, 0,
    )
    f32, bf16 = jnp.float32, jnp.bfloat16
    vmem, smem = pl.BlockSpec(memory_space=pltpu.VMEM), pl.BlockSpec(memory_space=pltpu.SMEM)
    anywhere = pl.BlockSpec(memory_space=pl.ANY)
    dma = pltpu.SemaphoreType.DMA

    def held(count, dtype):
        return pltpu.VMEM((count, size, width), dtype)

    primal, dual, weight = pl.pallas_call(
        functools.partial(kernel, n_row, n_col),
        out_shape=(
            jax.ShapeDtypeStruct((blocks_c, size, width), f32),
            jax.ShapeDtypeStruct((share, size, width), f32),
            jax.ShapeDtypeStruct((8, width), f32),
        ),
        in_specs=[smem, smem, smem, smem, anywhere, vmem, vmem, anywhere, vmem],
        out_specs=(vmem, vmem, vmem),
        scratch_shapes=[
            pltpu.VMEM((total, size, size), bf16),
            held(quarter, f32),
            held(ITERS * blocks_r, bf16),
            pltpu.VMEM((blocks_r, width, size), bf16),
            held(total, f32),
            held(ITERS * blocks_c, bf16),
            held(quarter, f32),
            held(ITERS * blocks_c, bf16),
            held(ITERS * blocks_c, bf16),
            held(ITERS * n_chip * share, f32),
            held(ITERS * n_chip * share, f32),
            held(ITERS * n_chip * share, bf16),
            held(share, f32),
            held(ITERS * n_chip * share, bf16),
            pltpu.VMEM(((ITERS + 1) * n_row, 8, width), f32),
            pltpu.VMEM(((ITERS + 1) * n_col, 8, width), f32),
            dma((2,)),
            dma((ITERS, n_chip)), dma((ITERS, n_col)), dma((ITERS, n_chip)),
            dma((ITERS, n_row)), dma((ITERS, n_row)),
            dma((ITERS, n_row)), dma((ITERS, n_row)),
            dma((n_row,)), dma((n_row,)),
            dma((ITERS, n_chip)), dma((ITERS, n_chip)),
            dma((ITERS, n_chip)), dma((ITERS, n_chip)),
            dma((ITERS + 1, n_row)), dma((ITERS + 1, n_row)),
            dma((ITERS + 1, n_col)), dma((ITERS + 1, n_col)),
        ],
        compiler_params=pltpu.CompilerParams(
            collective_id=0, has_side_effects=True, vmem_limit_bytes=54 * 2**20
        ),
        cost_estimate=pl.CostEstimate(
            flops=4 * ITERS * total * size * size * width,
            bytes_accessed=2 * total * size * size, transcendentals=0,
        ),
    )(
        plan_r, plan_c, ends_r, ends_c, tile_values, params,
        demand.reshape(share, size, width),
        primal_start.reshape(blocks_c, size, width),
        dual_start.reshape(share, size, width),
    )
    return primal.reshape(primal_start.shape), dual.reshape(dual_start.shape), weight[0]


def solution(mesh):
    return jax.shard_map(
        on_device,
        mesh=mesh,
        in_specs=(
            P("row", "col", None),
            P("row", "col"),
            P("row", "col"),
            P("col"),
            P(("row", "col"), None),
            P("col"),
            P("col"),
            P("col"),
            P("col", None),
            P(("row", "col"), None),
        ),
        out_specs=(P("col", None), P(("row", "col"), None), P()),
        check_vma=False,
    )
```

time: 545 us -> 174 us (0.32)
  waiting for transfers between devices: 177 us -> 0 us
  blocking collectives: 163 us -> 0 us
  Pallas kernels: 0 us -> 157 us
  local copies, waits for them, and re-layouts: 83.7 us -> 6.09 us
  matrix products: 76.9 us -> 0 us
  other arithmetic: 27.3 us -> 9.39 us
  between operations: 15 us -> 0.7 us
    psum x6 -> x0, blocking collectives: 163 us -> none  [the longest x2 78 us: on_device(): dual_sq = lax.psum(dual_local, ('row', 'col'))]
    pallas_call x0 -> x1, Pallas kernels: none -> 157 us  [on_device(): pl.pallas_call(functools.partial(kernel, n_row, n_col), out_shape=(jax.Sh...]
    psum x4 -> x0, waiting for transfers between devices: 143 us -> none  [the longest x2 113 us: on_device(): pushed = lax.psum(pushed_part, 'col')]
    dot_general x8 -> x0, matrix products: 76.9 us -> none  [the longest x2 26.4 us: local_transpose(): jnp.einsum('tij,tis->tjs', tile_values, pieces, preferred_element_type=jn...]
    dot_general x8 -> x0, local copies, waits for them, and re-layouts: 58.9 us -> none  [the longest x2 25.6 us: local_forward(): jnp.einsum('tij,tjs->tis', tile_values, pieces, preferred_element_type=jn...]
    all_gather x2 -> x0, waiting for transfers between devices: 32.8 us -> none  [the longest x1 32.8 us: on_device(): lax.all_gather(dual_start, 'col', axis=0, tiled=True)]
    gather x4 -> x0, local copies, waits for them, and re-layouts: 23.8 us -> none  [the longest x2 11.9 us: local_transpose(): pieces = dual_rows.reshape(count_rows, tile_size, width)[row_ids]]
    reduce_sum x6 -> x5, other arithmetic: 16.5 us -> 4.23 us  [the longest x2 1.77 us: schedule(): perm = jnp.sum(jnp.where(here, order[None, :], 0), axis=1)]
  transfers between devices with their start and end apart: 6 -> 0, of which waited for: 5 -> 0; matrix products, arithmetic and copies ran while one was open for 9% -> 0% of each run, Pallas kernels for 0% -> 0%
where the time goes in v1:
time: 174 us; the launch traced here: 173 us
  Pallas kernels  157 us (90%)
  other arithmetic  9.39 us (5%)
  local copies, waits for them, and re-layouts  6.09 us (4%)
    pallas_call x1, Pallas kernels, on_device(): pl.pallas_call(functools.partial(kernel, n_row, n_col), out_shape=(jax.Sh...  157 us
    unnamed x5, local copies, waits for them, and re-layouts  4.82 us

profile of v1, /device:TPU:0, one launch (start us, length us, event | category | flops | bytes accessed | tf_op | source)
XLA Modules:
  0.0 173.3 jit_solution(14898081994324091831)
XLA Ops:
  0.6 0.9 fusion.4
  1.6 0.9 fusion.5
  2.5 0.9 convert_reduce_fusion.1
  3.4 0.1 pad.3.clone
  3.5 1.0 select_reduce_fusion.1
  4.5 0.8 select_reduce_fusion.3
  5.3 0.6 pad_add_fusion
  5.9 0.8 convert_reduce_fusion.7
  6.7 0.8 convert_reduce_fusion.5
  7.4 0.6 pad_add_fusion.3.ends_c
  8.0 0.6 pad_add_fusion.2.ends_r
  8.6 0.8 add_select_fusion
  9.4 0.8 fusion.8
  10.2 1.0 copy.18.params
  11.2 157.1 %shard_map.121 = (f32[16,256,128]{2,1,0:T(8,128)}, f32[2,256,128]{2,1,0:T(8,128)}, f32[8,128]{1,0:T(8,128)}) custom-call(s32[3,96]{1,0:T(4,128)} %get-tuple-element.24.plan_r, s32[3,96]{1,0:T(4,128)} %get-tuple-element.25.plan_c, s32[2,16]{1,0:T(2,128)} %pad_add_fusion.2.ends_r, s32[2,16]{1,0:T(2,128)} %pad_add_fusion.3.ends_c, ...), custom_call_target="tpu_custom_call" | custom-call | flops 6442450944 | bytes 12582912 | tf_op jit(solution)/shard_map/pallas_call | solution.py:366
  168.3 1.2 slice_bitcast_fusion
  169.5 0.0 copy-start
  169.5 3.1 %copy.21 = f32[4096,128]{1,0:T(8,128)} copy(f32[4096,128]{1,0:T(8,128)} %bitcast.27) | data formatting | bytes 4194304
  172.6 0.0 copy-done
  172.6 0.7 copy.22
  (5 shorter events, 0.0 us)
Async XLA Ops:
  169.5 3.1 %copy-start = (f32[2,256,128]{2,1,0:T(8,128)S(1)}, f32[2,256,128]{2,1,0:T(8,128)}, u32[]{:S(2)}) copy-start(f32[2,256,128]{2,1,0:T(8,128)} %get-tuple-element.7) | copy-start | bytes 786436

commit v2 on v1

v2 whole, which is shorter than its diff:
```python
import functools
import jax
import jax.numpy as jnp
from jax import lax
from jax.experimental import pallas as pl
from jax.experimental.pallas import tpu as pltpu
from jax.sharding import PartitionSpec as P

ITERS = 2
CORES = 2
HALVES = 2
OTHER_BIT, KEEP_BIT, COUNT_BIT = 12, 24, 16

eps_norm = 1e-06
step_scale = 0.4
MESH = pl.DeviceIdType.MESH


def schedule(keys, others, count):
    total = keys.shape[1]
    order = jnp.arange(total, dtype=jnp.int32)
    same = (keys[:, None, :] == keys[:, :, None]) & (order[None, :] < order[:, None])[None]
    ahead = same | (keys[:, None, :] < keys[:, :, None])
    rank = jnp.sum(ahead.astype(jnp.int32), axis=2)
    keep = jnp.max(same.astype(jnp.int32), axis=2)
    code = order[None, :] + (others << OTHER_BIT) + (keep << KEEP_BIT)
    here = rank[:, None, :] == order[None, :, None]
    plan = jnp.sum(jnp.where(here, code[:, None, :], 0), axis=2)
    ids = jnp.arange(count, dtype=jnp.int32)[None, :, None]
    upto = (keys[:, None, :] <= ids).astype(jnp.int32)
    equal = (keys[:, None, :] == ids).astype(jnp.int32)
    return plan, jnp.sum(upto + (equal << COUNT_BIT), axis=2)


def kernel(
    n_row, n_col,
    plan, ends, tiles_any, params, demand, primal_any, dual_start,
    primal_out, dual_out, weight_out,
    tiles, primal_in, primal, wanted, dual, dual_rows, run, pull_out, pull_own, pull_in, mixed,
    pair_out, pair_in, push_out, push_own, push_in, final, norm_row, norm_col,
    load_sem, gather_send, gather_recv, pass_send, pull_send, pull_recv,
    mix_send, mix_recv, final_send, final_recv, pair_send, pair_recv,
    push_send, push_recv, nrow_send, nrow_recv, ncol_send, ncol_recv,
):
    i, j = lax.axis_index("row"), lax.axis_index("col")
    n_chip = n_col // CORES
    chip, core = lax.div(j, CORES), lax.rem(j, CORES)
    other_core = 1 - core
    partner = (i, chip * CORES + other_core)
    total, size = tiles.shape[0], tiles.shape[1]
    share, width = demand.shape[0], demand.shape[2]
    lanes = width // HALVES
    quarter = primal_in.shape[0]
    blocks_c = n_row * quarter
    blocks_r = n_col * share
    f32, bf16 = jnp.float32, jnp.bfloat16
    sends = []

    def remote(src, dst, send_sem, recv_sem, device):
        return pltpu.make_async_remote_copy(
            src_ref=src, dst_ref=dst, send_sem=send_sem, recv_sem=recv_sem,
            device_id=device, device_id_type=MESH,
        )

    def send(*args):
        copy = remote(*args)
        copy.start()
        sends.append(copy)

    row_peer = [lax.rem(i + d, n_row) for d in range(n_row)]
    col_peer = [lax.rem(j + d, n_col) for d in range(n_col)]
    chip_peer = [lax.rem(chip + d, n_chip) for d in range(n_chip)]

    load_tiles = pltpu.make_async_copy(tiles_any, tiles, load_sem.at[0])
    load_tiles.start()
    load_primal = pltpu.make_async_copy(
        primal_any.at[pl.ds(i * quarter, quarter)], primal_in, load_sem.at[1]
    )
    load_primal.start()

    barrier = pltpu.get_barrier_semaphore()
    for d in range(1, n_row):
        pl.semaphore_signal(barrier, inc=1, device_id=(row_peer[d], j), device_id_type=MESH)
    for d in range(1, n_col):
        pl.semaphore_signal(barrier, inc=1, device_id=(i, col_peer[d]), device_id_type=MESH)

    zero = jnp.zeros((lanes, 1), f32)

    def squares(value):
        return jnp.sum(value * value, axis=1, keepdims=True)

    def share_of(p, owner):
        return dual_rows[p].at[pl.ds(owner * share, share)]

    def gather_start(p):
        for d in range(1, n_chip):
            send(share_of(p, j), share_of(p, j), gather_send.at[p, d], gather_recv.at[p, j],
                 (i, chip_peer[d] * CORES + core))
        send(share_of(p, j), share_of(p, j), pass_send.at[p, 0], gather_recv.at[p, j], partner)

    def gather_finish(p):
        for d in range(1, n_chip):
            owner = chip_peer[n_chip - d] * CORES + core
            remote(share_of(p, owner), share_of(p, owner), gather_send.at[p, d],
                   gather_recv.at[p, owner], partner).wait_recv()
            send(share_of(p, owner), share_of(p, owner), pass_send.at[p, d],
                 gather_recv.at[p, owner], partner)
        for d in range(n_chip):
            owner = chip_peer[d] * CORES + other_core
            remote(share_of(p, owner), share_of(p, owner), pass_send.at[p, d],
                   gather_recv.at[p, owner], partner).wait_recv()

    def norm_start(p, first, second):
        lane = lax.broadcasted_iota(jnp.int32, (lanes, width), 1)
        laid = jnp.where(lane == 0, first, jnp.where(lane == 1, second, 0.0))
        square = jnp.concatenate([laid, jnp.zeros((width - lanes, width), f32)], axis=0)
        norm_row[p * n_row + i] = square.T[0:8, :]
        for d in range(1, n_row):
            slot = norm_row.at[p * n_row + i]
            send(slot, slot, nrow_send.at[p, d], nrow_recv.at[p, i], (row_peer[d], j))

    def norm_middle(p):
        for d in range(1, n_row):
            slot = norm_row.at[p * n_row + row_peer[d]]
            remote(slot, slot, nrow_send.at[p, d], nrow_recv.at[p, row_peer[d]],
                   (row_peer[d], j)).wait_recv()
        added = norm_row[p * n_row]
        for k in range(1, n_row):
            added = added + norm_row[p * n_row + k]
        norm_col[p * n_col + j] = added
        for d in range(1, n_col):
            slot = norm_col.at[p * n_col + j]
            send(slot, slot, ncol_send.at[p, d], ncol_recv.at[p, j], (i, col_peer[d]))

    def norm_finish(p):
        for d in range(1, n_col):
            slot = norm_col.at[p * n_col + col_peer[d]]
            remote(slot, slot, ncol_send.at[p, d], ncol_recv.at[p, col_peer[d]],
                   (i, col_peer[d])).wait_recv()
        added = norm_col[p * n_col]
        for k in range(1, n_col):
            added = added + norm_col[p * n_col + k]
        square = jnp.concatenate([added, jnp.zeros((width - 8, width), f32)], axis=0).T
        return square[0:lanes, 0:1], square[0:lanes, 1:2]

    weight = [None] * HALVES
    primal_sq = [None] * HALVES

    def begin(b, carry):
        rows = dual_start[b].T
        right = demand[b].T
        out = []
        for h in range(HALVES):
            part = rows[h * lanes:(h + 1) * lanes, :]
            dual[h * share + b] = part
            dual_rows[h][j * share + b] = part.astype(bf16)
            part = right[h * lanes:(h + 1) * lanes, :]
            wanted[h * share + b] = part
            out.append(carry[h] + squares(part))
        return tuple(out)

    demand_sq = lax.fori_loop(0, share, begin, (zero,) * HALVES)
    pl.semaphore_wait(barrier, n_row + n_col - 2)
    cost_sq = jnp.broadcast_to(squares(params[0:1, :]), (lanes, 1))
    for h in range(HALVES):
        gather_start(h)
        norm_start(h, demand_sq[h], cost_sq)
    load_primal.wait()

    def turn(b, carry):
        rows = primal_in[b].T
        for h in range(HALVES):
            primal[h * quarter + b] = rows[h * lanes:(h + 1) * lanes, :]
        return carry

    lax.fori_loop(0, quarter, turn, 0)
    load_tiles.wait()

    def multiply(which, source, dims):
        def one(n, before):
            code = plan[which, n]
            tile = code & ((1 << OTHER_BIT) - 1)
            other = (code >> OTHER_BIT) & ((1 << (KEEP_BIT - OTHER_BIT)) - 1)
            added = lax.dot_general(source[other], tiles[tile], (dims, ((), ())),
                                    preferred_element_type=f32)
            added = added + jnp.where((code >> KEEP_BIT) == 1, before, 0.0)
            run[n] = added
            return added

        lax.fori_loop(0, total, one, jnp.zeros((lanes, size), f32), unroll=8)

    def summed(which, block):
        code = ends[which, block]
        last = jnp.maximum((code & ((1 << COUNT_BIT) - 1)) - 1, 0)
        return jnp.where((code >> COUNT_BIT) > 0, run[last], 0.0)

    def pull(t, h):
        p = t * HALVES + h
        gather_finish(p)
        norm_middle(p)
        multiply(1, dual_rows[p], ((1,), (0,)))
        for d in range(1, n_row):
            dest = row_peer[d]

            def pack(b, carry):
                at = dest * quarter + b
                pull_out[p * blocks_c + at] = summed(1, at).astype(bf16)
                return carry

            lax.fori_loop(0, quarter, pack, 0)
            send(pull_out.at[pl.ds(p * blocks_c + dest * quarter, quarter)],
                 pull_in.at[pl.ds(p * blocks_c + i * quarter, quarter)],
                 pull_send.at[p, d], pull_recv.at[p, i], (dest, j))

        def own(b, carry):
            pull_own[h * quarter + b] = summed(1, i * quarter + b)
            return carry

        lax.fori_loop(0, quarter, own, 0)

    def new_weight(p, h):
        dual_all, primal_all = norm_finish(p)
        if p < HALVES:
            weight[h] = jnp.sqrt(primal_all + eps_norm) / jnp.sqrt(dual_all + eps_norm)
        else:
            weight[h] = jnp.sqrt(
                weight[h] * jnp.sqrt((dual_all + eps_norm) / (primal_all + eps_norm)))

    def update_primal(t, h):
        p = t * HALVES + h
        new_weight(p, h)
        step = step_scale / weight[h]
        for d in range(1, n_row):
            origin = row_peer[n_row - d]
            slot = pull_in.at[pl.ds(p * blocks_c + origin * quarter, quarter)]
            remote(slot, slot, pull_send.at[p, d], pull_recv.at[p, origin],
                   (origin, j)).wait_recv()

        def one(b, carry):
            pulled = pull_own[h * quarter + b]
            for d in range(1, n_row):
                pulled = pulled + pull_in[
                    p * blocks_c + row_peer[d] * quarter + b].astype(f32)
            at = pl.ds(pl.multiple_of(b * size, size), size)
            old = primal[h * quarter + b]
            value = old - step * (params[0:1, at] - pulled)
            new = jnp.minimum(jnp.maximum(value, params[1:2, at]), params[2:3, at])
            mixed[p][i * quarter + b] = (2.0 * new - old).astype(bf16)
            if t == ITERS - 1:
                final[h * blocks_c + i * quarter + b] = new
            else:
                primal[h * quarter + b] = new
            return carry + squares(new - old)

        primal_sq[h] = lax.fori_loop(0, quarter, one, zero)
        mine = mixed[p].at[pl.ds(i * quarter, quarter)]
        for d in range(1, n_row):
            send(mine, mine, mix_send.at[p, d], mix_recv.at[p, i], (row_peer[d], j))

    def send_final(h):
        mine = final.at[pl.ds(h * blocks_c + i * quarter, quarter)]
        for d in range(1, n_row):
            send(mine, mine, final_send.at[h, d], final_recv.at[h, i], (row_peer[d], j))

    def mixed_wait(p):
        for d in range(1, n_row):
            origin = row_peer[n_row - d]
            slot = mixed[p].at[pl.ds(origin * quarter, quarter)]
            remote(slot, slot, mix_send.at[p, d], mix_recv.at[p, origin],
                   (origin, j)).wait_recv()

    order = [*range(1, n_chip), 0]

    def push(t, h):
        p = t * HALVES + h
        mixed_wait(p)
        if t == ITERS - 1:
            send_final(h)
        multiply(0, mixed[p], ((1,), (1,)))

        def part(ref, owner_chip):
            return ref.at[pl.ds((p * n_chip + owner_chip) * share, share)]

        for d in order:
            dest = chip_peer[d]

            def pack(b, carry):
                pair_out[(p * n_chip + dest) * share + b] = summed(
                    0, (dest * CORES + other_core) * share + b)
                return carry

            lax.fori_loop(0, share, pack, 0)
            send(part(pair_out, dest), part(pair_in, dest), pair_send.at[p, d],
                 pair_recv.at[p, dest], partner)
        for d in order:
            dest = chip_peer[d]
            slot = part(pair_in, dest)
            remote(slot, slot, pair_send.at[p, d], pair_recv.at[p, dest], partner).wait_recv()

            def pack_push(b, carry):
                at = (p * n_chip + dest) * share + b
                value = summed(0, (dest * CORES + core) * share + b) + pair_in[at]
                if d == 0:
                    push_own[h * share + b] = value
                else:
                    push_out[at] = value.astype(bf16)
                return carry

            lax.fori_loop(0, share, pack_push, 0)
            if d != 0:
                send(part(push_out, dest), part(push_in, chip), push_send.at[p, d],
                     push_recv.at[p, chip], (i, dest * CORES + core))

    def update_dual(t, h):
        p = t * HALVES + h
        step = step_scale * weight[h]
        for d in range(1, n_chip):
            origin = chip_peer[n_chip - d]
            slot = push_in.at[pl.ds((p * n_chip + origin) * share, share)]
            remote(slot, slot, push_send.at[p, d], push_recv.at[p, origin],
                   (i, origin * CORES + core)).wait_recv()

        def one(b, carry):
            pushed = push_own[h * share + b]
            for d in range(1, n_chip):
                pushed = pushed + push_in[
                    (p * n_chip + chip_peer[d]) * share + b].astype(f32)
            change = step * (wanted[h * share + b] - pushed)
            new = dual[h * share + b] + change
            dual[h * share + b] = new
            if t < ITERS - 1:
                dual_rows[p + HALVES][j * share + b] = new.astype(bf16)
            return carry + squares(change)

        dual_sq = lax.fori_loop(0, share, one, zero)
        if t < ITERS - 1:
            gather_start(p + HALVES)
        norm_start(p + HALVES, dual_sq, primal_sq[h])

    for t in range(ITERS):
        for step in (pull, update_primal, push, update_dual):
            for h in range(HALVES):
                step(t, h)

    def together(ref, stride, b):
        return jnp.concatenate([ref[h * stride + b] for h in range(HALVES)], axis=0).T

    for h in range(HALVES):
        norm_middle(ITERS * HALVES + h)

    def finish_dual(b, carry):
        dual_out[b] = together(dual, share, b)
        return carry

    lax.fori_loop(0, share, finish_dual, 0)
    for d in range(n_row):
        origin = row_peer[n_row - d] if d else i
        if d:
            for h in range(HALVES):
                slot = final.at[pl.ds(h * blocks_c + origin * quarter, quarter)]
                remote(slot, slot, final_send.at[h, d], final_recv.at[h, origin],
                       (origin, j)).wait_recv()

        def finish_primal(b, carry):
            primal_out[origin * quarter + b] = together(final, blocks_c, origin * quarter + b)
            return carry

        lax.fori_loop(0, quarter, finish_primal, 0)
    for h in range(HALVES):
        new_weight(ITERS * HALVES + h, h)
    column = jnp.concatenate(weight, axis=0)
    weight_out[...] = jnp.broadcast_to(column, (width, width)).T[0:1, :]
    for copy in sends:
        copy.wait_send()


def on_device(
    tile_values, tile_rows, tile_cols, objective, demand, lower_bound, bound_span, bound_types,
    primal_start, dual_start,
):
    n_row, n_col = lax.axis_size("row"), lax.axis_size("col")
    total, size = tile_values.shape[0], tile_values.shape[1]
    width = demand.shape[1]
    share = dual_start.shape[0] // size
    blocks_r = share * n_col
    blocks_c = primal_start.shape[0] // size
    quarter = blocks_c // n_row
    n_chip = n_col // CORES
    keys = jnp.stack([tile_rows.reshape(-1), tile_cols.reshape(-1)])
    plan, ends = schedule(keys, keys[::-1], max(blocks_r, blocks_c))
    low = jnp.where(bound_types == 0, -jnp.inf, lower_bound)
    high = jnp.where(bound_types == 2, lower_bound + bound_span, jnp.inf)
    params = lax.dynamic_slice_in_dim(
        jnp.stack([objective, low, high]),
        lax.axis_index("row") * quarter * size, quarter * size, 1,
    )
    f32, bf16 = jnp.float32, jnp.bfloat16
    vmem, smem = pl.BlockSpec(memory_space=pltpu.VMEM), pl.BlockSpec(memory_space=pltpu.SMEM)
    anywhere = pl.BlockSpec(memory_space=pl.ANY)
    dma = pltpu.SemaphoreType.DMA
    phases = ITERS * HALVES
    norms = phases + HALVES

    def held(count, dtype):
        return pltpu.VMEM((count, width // HALVES, size), dtype)

    primal, dual, weight = pl.pallas_call(
        functools.partial(kernel, n_row, n_col),
        out_shape=(
            jax.ShapeDtypeStruct((blocks_c, size, width), f32),
            jax.ShapeDtypeStruct((share, size, width), f32),
            jax.ShapeDtypeStruct((1, width), f32),
        ),
        in_specs=[smem, smem, anywhere, vmem, vmem, anywhere, vmem],
        out_specs=(vmem, vmem, vmem),
        scratch_shapes=[
            pltpu.VMEM((total, size, size), bf16),
            pltpu.VMEM((quarter, size, width), f32),
            held(HALVES * quarter, f32),
            held(HALVES * share, f32),
            held(HALVES * share, f32),
            (held(blocks_r, bf16),) * phases,
            held(total, f32),
            held(phases * blocks_c, bf16),
            held(HALVES * quarter, f32),
            held(phases * blocks_c, bf16),
            (held(blocks_c, bf16),) * phases,
            held(phases * n_chip * share, f32),
            held(phases * n_chip * share, f32),
            held(phases * n_chip * share, bf16),
            held(HALVES * share, f32),
            held(phases * n_chip * share, bf16),
            held(HALVES * blocks_c, f32),
            pltpu.VMEM((norms * n_row, 8, width), f32),
            pltpu.VMEM((norms * n_col, 8, width), f32),
            dma((2,)),
            dma((phases, n_chip)), dma((phases, n_col)), dma((phases, n_chip)),
            dma((phases, n_row)), dma((phases, n_row)),
            dma((phases, n_row)), dma((phases, n_row)),
            dma((HALVES, n_row)), dma((HALVES, n_row)),
            dma((phases, n_chip)), dma((phases, n_chip)),
            dma((phases, n_chip)), dma((phases, n_chip)),
            dma((norms, n_row)), dma((norms, n_row)),
            dma((norms, n_col)), dma((norms, n_col)),
        ],
        compiler_params=pltpu.CompilerParams(
            collective_id=0, has_side_effects=True, vmem_limit_bytes=54 * 2**20
        ),
        cost_estimate=pl.CostEstimate(
            flops=4 * ITERS * total * size * size * width,
            bytes_accessed=2 * total * size * size, transcendentals=0,
        ),
    )(
        plan, ends, tile_values, params,
        demand.reshape(share, size, width),
        primal_start.reshape(blocks_c, size, width),
        dual_start.reshape(share, size, width),
    )
    return primal.reshape(primal_start.shape), dual.reshape(dual_start.shape), weight.reshape(width)


def solution(mesh):
    return jax.shard_map(
        on_device,
        mesh=mesh,
        in_specs=(
            P("row", "col", None),
            P("row", "col"),
            P("row", "col"),
            P("col"),
            P(("row", "col"), None),
            P("col"),
            P("col"),
            P("col"),
            P("col", None),
            P(("row", "col"), None),
        ),
        out_specs=(P("col", None), P(("row", "col"), None), P()),
        check_vma=False,
    )
```

time: 174 us -> 142 us (0.82)
  Pallas kernels: 157 us -> 132 us
  other arithmetic: 9.39 us -> 4.37 us
  local copies, waits for them, and re-layouts: 6.09 us -> 4.34 us
    pallas_call x1, Pallas kernels: 157 us -> 132 us  [on_device(): pl.pallas_call(functools.partial(kernel, n_row, n_col), out_shape=(jax.Sh...]
    reduce_sum x5 -> x3, other arithmetic: 4.23 us -> 1.53 us  [the longest x1 0.68 us: schedule(): plan = jnp.sum(jnp.where(here, code[:, None, :], 0), axis=2)]
    reduce_or x2 -> x0, other arithmetic: 1.83 us -> none  [schedule(): jnp.any((keys[None, :] == keys[:, None]) & (order[None, :] < order[:, Non...]
    unnamed x5 -> x7, local copies, waits for them, and re-layouts: 4.82 us -> 4.31 us
where the time goes in v2:
time: 142 us
  Pallas kernels  132 us (93%)
  other arithmetic  4.37 us (3%)
  local copies, waits for them, and re-layouts  4.34 us (3%)
    pallas_call x1, Pallas kernels, on_device(): pl.pallas_call(functools.partial(kernel, n_row, n_col), out_shape=(jax.Sh...  132 us
    unnamed x7, local copies, waits for them, and re-layouts  4.31 us

profile of v2, /device:TPU:0, one launch (start us, length us, event | category | flops | bytes accessed | tf_op | source)
XLA Modules:
  0.0 141.6 jit_solution(6068979312659034475)
XLA Ops:
  0.6 0.7 pad_add_fusion
  1.3 0.6 add_reduce_fusion.ends
  2.0 0.2 convert_reduce_fusion.1
  2.2 0.7 select_reduce_fusion.plan
  2.9 0.8 add_select_fusion
  3.7 1.4 fusion.1.params
  5.0 132.2 %shard_map.121 = (f32[16,256,128]{2,1,0:T(8,128)}, f32[2,256,128]{2,1,0:T(8,128)}, f32[1,128]{1,0:T(1,128)}) custom-call(s32[2,96]{1,0:T(2,128)} %select_reduce_fusion.plan, s32[2,16]{1,0:T(2,128)} %add_reduce_fusion.ends, bf16[96,256,256]{2,1,0:T(8,128)(2,1)} %tiles_any.1, f32[3,1024]{1,0:T(4,128)} %fusion.1.params, f32[2,256,128]{2,1,0:T(8,128)} %bitcast.19, ...), custom_call_target="tpu_custom_call" | custom-call | flops 6442450944 | bytes 12582912 | tf_op jit(solution)/shard_map/pallas_call | solution.py:407
  137.2 0.0 copy-start
  137.2 0.0 copy-start.1
  137.2 3.1 %copy.16 = f32[4096,128]{1,0:T(8,128)} copy(f32[4096,128]{1,0:T(8,128)} %bitcast.11) | data formatting | bytes 4194304
  140.3 0.0 copy-done
  140.3 0.7 copy.17
  141.0 0.0 copy-done.1
  141.0 0.5 copy.18
  (3 shorter events, 0.0 us)
Async XLA Ops:
  137.2 3.1 %copy-start = (f32[2,256,128]{2,1,0:T(8,128)S(1)}, f32[2,256,128]{2,1,0:T(8,128)}, u32[]{:S(2)}) copy-start(f32[2,256,128]{2,1,0:T(8,128)} %get-tuple-element.7) | copy-start | bytes 786436
  137.2 3.8 %copy-start.1 = (f32[1,128]{1,0:T(1,128)S(1)}, f32[1,128]{1,0:T(1,128)}, u32[]{:S(2)}) copy-start(f32[1,128]{1,0:T(1,128)} %get-tuple-element.8) | copy-start | bytes 1540
